TPU v7x, 256 devices: a whole 4x4x8 slice. The times are simulated.
256 devices in a mesh: expert: 8 (over z), vocab: 8 (over x, core), batch: 4 (over y).
Axes of the slice: x: 4, y: 4, z: 8, core: 2. Of those that a mesh axis runs over, the one named last changes fastest.
Arguments:
- resid: bfloat16 [4, 512, 6144], P('batch', ('expert', 'vocab')), may hold values from -6 to 6
- moe_gain: float32 [6144], replicated, may hold values from 0.25 to 2.5
- final_gain: float32 [6144], replicated, may hold values from 0.5 to 1.5
- router: bfloat16 [6144, 8], replicated, may hold values from -0.078125 to 0.078125
- w_gate: bfloat16 [8, 6144, 8192], P('expert', None, ('vocab', 'batch')), may hold values from -0.078125 to 0.078125
- w_up: bfloat16 [8, 6144, 8192], P('expert', None, ('vocab', 'batch')), may hold values from -0.078125 to 0.078125
- w_down: bfloat16 [8, 8192, 6144], P('expert', ('vocab', 'batch')), may hold values from -0.0625 to 0.0625
- lm_head: bfloat16 [16384, 6144], P(('expert', 'vocab')), may hold values from -6 to 6
- expert_ids: int32 [4, 512, 2], P('batch', ('expert', 'vocab')), may hold values from 0 to 7, all different within a row; in each aligned block of 8 rows (0 to 7, 8 to 15, ..., all dimensions but the last counted through in order) at most 3 rows name the same one
- target_ids: int32 [4, 512], P('batch'), may hold values from 0 to 16383
- choice_len: int32 [4, 16], P('batch'), may hold values from 1 to 64, 512 in all within a row
- choice_question: int32 [4, 16], P('batch'), may hold values from 0 to 3, as said below
Outputs:
- token_logprob: float32 [4, 512], P('batch', ('expert', 'vocab'))
- choice_prob: float32 [4, 16], P('batch')
Inputs may be any that keep to these rules, and one draw needn't show every extreme that they name: `expert_ids`: A token's 2 experts differ; the rows of one device name each expert at most 3 times. `choice_len`: each group's lengths sum to 512. `choice_question`: in each group every question number appears exactly four times.
All inputs are finite; a program needn't handle non-finite values.
Results may differ from a plain program's by a relative error of at most 0.019.
Values may be sent and summed in bfloat16 or wider, within the bound.
No kernel may reach another device: no remote copies, remote signals or barrier semaphores. Data moves between devices by JAX's collectives and lax.ppermute only.
A program may use at most 128 MiB of HBM per device.

v0:
```python
import jax
import jax.numpy as jnp
from jax import lax
from jax.sharding import PartitionSpec as P

epsilon = 1e-05


def copy_for_each(array, axis):
    peers = lax.axis_size(axis)
    return lax.all_to_all(
        jnp.broadcast_to(array[None], (peers, *array.shape)), axis, 0, 0, tiled=True
    )


def gathered_once(array, axis):
    leaves = jax.tree.leaves(array)
    order = sorted(range(len(leaves)), key=lambda k: -leaves[k].size)
    width = (1, *leaves[order[0]].shape)[-1]
    lines = [
        jnp.pad(leaves[k].reshape(-1), (0, -leaves[k].size % width)).reshape(-1, width)
        for k in order
    ]
    both, at, found = (copy_for_each(jnp.concatenate(lines), axis), 0, {})
    for k, line in zip(order, lines):
        slab = both[:, at : at + len(line)].reshape(len(both), -1)
        found[k] = slab[:, : leaves[k].size].reshape(-1, *leaves[k].shape)
        at += len(line)
    numbers = iter(range(len(leaves)))
    return jax.tree.map(lambda _: found[next(numbers)], array)


def joined_by_halves(pieces, combine):
    while len(jax.tree.leaves(pieces)[0]) > 1:
        pieces = jax.vmap(combine)(
            *(jax.tree.map(lambda part: part[side::2], pieces) for side in (0, 1))
        )
    return jax.tree.map(lambda part: part[0], pieces)


def joined_all(array, axis, combine):
    pieces = gathered_once(array, axis)
    return joined_by_halves(pieces, combine)


def rms_scale(values, gain):
    mean_square = jnp.mean(values * values, axis=-1, keepdims=True)
    return values * lax.rsqrt(mean_square + epsilon) * gain


def route_gates(router_logit, route_ids):
    expert_count = router_logit.shape[1]
    matches = route_ids[:, :, None] == jnp.arange(expert_count, dtype=jnp.int32)[None, None, :]
    picked = jnp.sum(jnp.where(matches, router_logit[:, None, :], 0.0), axis=2)
    return 1.0 / jnp.sum(jnp.exp(picked[:, None, :] - picked[:, :, None]), axis=2)


def expand_rows(block_rows, gate_cols, up_cols):
    gate_part = jnp.dot(block_rows, gate_cols, preferred_element_type=jnp.float32)
    up_part = jnp.dot(block_rows, up_cols, preferred_element_type=jnp.float32)
    return (jax.nn.silu(gate_part) * up_part).astype(jnp.bfloat16)


def choice_member(lengths, positions):
    ends = jnp.cumsum(lengths, dtype=jnp.int32)
    starts = ends - lengths
    return (positions[None, :] >= starts[:, None]) & (positions[None, :] < ends[:, None])


def choice_softmax(choice_total, lengths, questions):
    average = choice_total / lengths.astype(jnp.float32)
    same_question = questions[:, None] == questions[None, :]
    question_top = jnp.max(jnp.where(same_question, average[None, :], -jnp.inf), axis=1)
    raised = jnp.exp(average - question_top)
    denominator = jnp.sum(jnp.where(same_question, raised[None, :], 0.0), axis=1)
    return raised / denominator


def merge_stats(first, second):
    top_value = jnp.maximum(first[0], second[0])
    summed = first[1] * jnp.exp(first[0] - top_value) + second[1] * jnp.exp(second[0] - top_value)
    return (top_value, summed, first[2] + second[2])


def on_device(
    resid,
    moe_gain,
    final_gain,
    router,
    w_gate,
    w_up,
    w_down,
    lm_head,
    expert_ids,
    target_ids,
    choice_len,
    choice_question,
):
    stream = resid[0].astype(jnp.float32)
    token_count, model_width = stream.shape
    normed_in = rms_scale(stream, moe_gain).astype(jnp.bfloat16)
    router_logit = jnp.dot(normed_in, router, preferred_element_type=jnp.float32)
    route_ids = expert_ids[0]
    route_count = route_ids.shape[1]
    gate_weights = route_gates(router_logit, route_ids)
    expert_count = lax.axis_size("expert")
    bucket_size = max(2, (token_count * route_count + expert_count - 1) // expert_count + 1)
    flat_ids = route_ids.reshape(-1)
    expert_match = (flat_ids[:, None] == jnp.arange(expert_count, dtype=jnp.int32)[None, :]).astype(
        jnp.int32
    )
    earlier = jnp.cumsum(expert_match, axis=0, dtype=jnp.int32) - expert_match
    slot_index = flat_ids * bucket_size + jnp.sum(earlier * expert_match, axis=1)
    slot_match = (
        slot_index[:, None] == jnp.arange(expert_count * bucket_size, dtype=jnp.int32)[None, :]
    ).astype(jnp.float32)
    slot_match = slot_match.reshape(token_count, route_count, -1)
    dispatch = jnp.sum(slot_match, axis=1).astype(jnp.bfloat16)
    combine_weights = jnp.sum(slot_match * gate_weights[:, :, None], axis=1)
    buckets = lax.dot_general(
        dispatch, normed_in, (((0,), (0,)), ((), ())), preferred_element_type=jnp.float32
    )
    buckets = buckets.astype(jnp.bfloat16).reshape(expert_count, bucket_size, model_width)
    gate_cols = w_gate[0]
    up_cols = w_up[0]
    down_rows = w_down[0]
    arrived = lax.all_to_all(buckets, "expert", split_axis=0, concat_axis=0, tiled=True).reshape(
        -1, model_width
    )
    hidden = expand_rows(
        lax.all_gather(arrived, ("vocab", "batch"), axis=0, tiled=True), gate_cols, up_cols
    )
    expert_sum = lax.psum_scatter(
        jnp.dot(hidden, down_rows, preferred_element_type=jnp.float32).astype(jnp.bfloat16),
        ("vocab", "batch"),
        scatter_dimension=0,
        tiled=True,
    )
    outgoing = expert_sum.reshape(expert_count, bucket_size, model_width)
    returned = lax.all_to_all(outgoing, "expert", split_axis=0, concat_axis=0, tiled=True)
    returned_rows = returned.reshape(-1, model_width).astype(jnp.float32)
    mixed_rows = stream + jnp.dot(combine_weights, returned_rows)
    normed_out = rms_scale(mixed_rows, final_gain).astype(jnp.bfloat16)
    head_index = lax.axis_index(("expert", "vocab"))
    vocab_share = lm_head.shape[0]
    vocab_ids = jnp.arange(vocab_share, dtype=jnp.int32) + head_index * vocab_share
    targets = target_ids[0]
    group_tokens = targets.shape[0]
    logits = lax.dot_general(
        lax.all_gather(normed_out, ("expert", "vocab"), axis=0, tiled=True),
        lm_head,
        (((1,), (1,)), ((), ())),
        preferred_element_type=jnp.float32,
    )
    block_top = jnp.max(logits, axis=1)
    block_sum = jnp.sum(jnp.exp(logits - block_top[:, None]), axis=1)
    block_hit = jnp.sum(jnp.where(targets[:, None] == vocab_ids[None, :], logits, 0.0), axis=1)
    fresh = (block_top, block_sum, block_hit)
    largest, spread_sum, chosen = tuple((fresh[slot] for slot in range(3)))
    lengths = choice_len[0]
    questions = choice_question[0]
    own_first = head_index * token_count
    group_positions = jnp.arange(group_tokens, dtype=jnp.int32)
    best, summed, target_sum = joined_all(
        (largest, spread_sum, chosen), ("expert", "vocab"), merge_stats
    )
    group_logprob = target_sum - (best + jnp.log(summed))
    choice_total = jnp.sum(
        jnp.where(choice_member(lengths, group_positions), group_logprob[None, :], 0.0), axis=1
    )
    own_logprob = lax.dynamic_slice_in_dim(group_logprob, own_first, token_count, 0)
    choice_prob = choice_softmax(choice_total, lengths, questions)
    return (own_logprob.reshape(1, -1), choice_prob.reshape(1, -1))


def solution(mesh):
    return jax.shard_map(
        on_device,
        mesh=mesh,
        in_specs=(
            P("batch", ("expert", "vocab"), None),
            P(),
            P(),
            P(),
            P("expert", None, ("vocab", "batch")),
            P("expert", None, ("vocab", "batch")),
            P("expert", ("vocab", "batch"), None),
            P(("expert", "vocab"), None),
            P("batch", ("expert", "vocab"), None),
            P("batch", None),
            P("batch", None),
            P("batch", None),
        ),
        out_specs=(P("batch", ("expert", "vocab")), P("batch", None)),
        check_vma=False,
    )
```

profile of v0, /device:TPU:1, one launch (start us, length us, event | category | flops | bytes accessed | tf_op | source)
XLA Modules:
  0.0 376.1 jit_solution(1491115489635027238)
XLA Ops:
  7.2 0.9 copy.31
  8.1 0.1 eq.72
  8.2 0.1 fusion.28
  8.3 0.2 select_reduce_fusion.4
  8.5 0.1 reduce_sum.106
  8.6 0.1 copy.32
  8.7 0.7 multiply_add_fusion.5
  9.4 1.1 fusion.19
  10.4 1.2 fusion.24
  11.6 0.8 select_reduce_fusion.3
  12.5 0.1 convert_reduce_fusion
  12.6 1.9 convolution_convert_fusion.1
  14.5 1.1 reshape.128
  15.6 22.4 %all_to_all.15 = bf16[8,3,6144]{2,1,0:T(4,128)(2,1)} all-to-all(bf16[8,3,6144]{2,1,0:T(4,128)(2,1)S(1)} %reshape.128), channel_id=1, replica_groups=mesh['expert'=8,'vocab'=8,'batch'=4] {'expert'}, dimensions={0} | all-to-all | bytes 589824 | tf_op jit(solution)/shard_map/all_to_all | solution.py:127
  38.1 2.0 reshape.129
  40.0 0.0 reduce-scatter.2.cloned.1.call-start
  40.1 58.8 %all-gather.3.cloned.1.call-done = bf16[768,6144]{1,0:T(8,128)(2,1)} async-done(((bf16[24,6144]{1,0:T(8,128)(2,1)}), bf16[768,6144]{1,0:T(8,128)(2,1)}) %all-gather.3.cloned.1.call-update) | async-done | bytes 9437200 | tf_op jit(solution)/shard_map/all_gather | solution.py:131
  98.9 8.1 %fusion.3 = f32[768,256]{1,0:T(8,128)} fusion(bf16[768,6144]{1,0:T(8,128)(2,1)} %all-gather.3.cloned.1.call-done, bf16[1,6144,256]{2,1,0:T(8,128)(2,1)} %param.16), kind=kOutput, calls=%fused_computation.6 | convolution fusion | flops 2415919104 | bytes 13369344 | tf_op jit(solution)/shard_map/dot_general | solution.py:59
  106.9 19.4 %convolution_convert_fusion = bf16[768,6144]{1,0:T(8,128)(2,1)} fusion(bf16[1,256,6144]{2,1,0:T(8,128)(2,1)S(1)} %copy-done, bf16[768,6144]{1,0:T(8,128)(2,1)} %all-gather.3.cloned.1.call-done, bf16[1,6144,256]{2,1,0:T(8,128)(2,1)} %param.17, f32[768,256]{1,0:T(8,128)} %fusion.3), kind=kOutput, calls=%fused_computation | convolution fusion | flops 4837736448 | bytes 25952256 | tf_op jit(solution)/shard_map/dot_general | solution.py:134
  126.3 0.0 all-gather.5.cloned.1.call-start
  126.4 100.8 %reduce-scatter.2.cloned.1.call-done = bf16[24,6144]{1,0:T(8,128)(2,1)} async-done(((bf16[768,6144]{1,0:T(8,128)(2,1)}), bf16[24,6144]{1,0:T(8,128)(2,1)}) %reduce-scatter.2.cloned.1.call-update) | async-done | bytes 294928 | tf_op jit(solution)/shard_map/reduce_scatter | solution.py:133
  227.2 1.1 reshape.130
  228.4 18.1 %all_to_all.16 = bf16[8,3,6144]{2,1,0:T(4,128)(2,1)} all-to-all(bf16[8,3,6144]{2,1,0:T(4,128)(2,1)S(1)} %reshape.130), channel_id=1, replica_groups=mesh['expert'=8,'vocab'=8,'batch'=4] {'expert'}, dimensions={0} | all-to-all | bytes 589824 | tf_op jit(solution)/shard_map/all_to_all | solution.py:140
  246.5 1.2 reshape.131
  247.7 1.2 multiply_reduce_fusion
  248.9 1.5 multiply_convert_fusion
  250.5 79.1 %all-gather.5.cloned.1.call-done = bf16[512,6144]{1,0:T(8,128)(2,1)} async-done(((bf16[8,6144]{1,0:T(8,128)(2,1)}), bf16[512,6144]{1,0:T(8,128)(2,1)}) %all-gather.5.cloned.1.call-update) | async-done | bytes 6291472 | tf_op jit(solution)/shard_map/all_gather | solution.py:150
  329.6 5.5 %fusion.37 = (f32[512]{0:T(512)S(1)}, f32[512,256]{0,1:T(8,128)S(1)}) fusion(bf16[512,6144]{1,0:T(8,128)(2,1)} %all-gather.5.cloned.1.call-done, bf16[256,6144]{1,0:T(8,128)(2,1)} %param.19), kind=kOutput, calls=%fused_computation.74 | convolution fusion | flops 1610743296 | bytes 9963520 | tf_op jit(solution)/shard_map/dot_general | solution.py:149
  335.2 0.1 exponential_reduce_fusion
  335.3 0.9 broadcast_in_dim.84
  336.2 5.9 %all-to-all-start.2 = ((f32[64,3,512]{2,1,0:T(4,128)}), f32[64,3,512]{2,1,0:T(4,128)}, u32[]{:S(2)}, u32[]{:S(2)}) async-start(f32[64,3,512]{2,1,0:T(4,128)} %broadcast_in_dim.84), calls=%async_computation.3 | async-start | bytes 1048576 | tf_op jit(solution)/shard_map/all_to_all | solution.py:11
  342.1 0.1 copy.35
  342.2 0.1 reduce
  342.3 0.5 bitcast_subtract_fusion.1
  342.8 16.9 %all-to-all-done.2 = f32[64,3,512]{2,1,0:T(4,128)} async-done(((f32[64,3,512]{2,1,0:T(4,128)}), f32[64,3,512]{2,1,0:T(4,128)}, u32[]{:S(2)}, u32[]{:S(2)}) %all-to-all-start.2) | async-done | bytes 393248 | tf_op jit(solution)/shard_map/all_to_all | solution.py:11
  359.7 1.8 fusion.36
  361.5 0.6 slice.124
  362.1 0.6 slice.125
  362.8 0.9 add.97
  363.9 0.6 slice.138
  364.6 0.6 slice.137
  365.2 0.9 multiply_add_fusion
  366.6 0.6 constant_dynamic-slice_fusion
  367.2 0.8 select_reduce_fusion.1
  368.0 0.7 bitcast_divide_fusion.1
  368.7 0.2 fusion.26
  368.9 0.2 fusion.27
  369.1 0.5 bitcast_divide_fusion
  (58 shorter events, 1.0 us)
Async XLA Ops:
  7.2 99.8 %copy-start = (bf16[1,256,6144]{2,1,0:T(8,128)(2,1)S(1)}, bf16[1,256,6144]{2,1,0:T(8,128)(2,1)}, u32[]{:S(2)}) copy-start(bf16[1,256,6144]{2,1,0:T(8,128)(2,1)} %param.18) | copy-start | bytes 9437188
  7.2 91.7 %all-gather.3.cloned.1.call-start = ((), (), s32[]{:S(2)}) async-start(), calls=%async_computation.4 | async-start | bytes 9732096 | tf_op jit(solution)/shard_map/all_gather | solution.py:131
  40.0 187.2 %reduce-scatter.2.cloned.1.call-start = ((), (), s32[]{:S(2)}) async-start(), calls=%async_computation.5 | async-start | bytes 9732096 | tf_op jit(solution)/shard_map/reduce_scatter | solution.py:133
  126.3 203.3 %all-gather.5.cloned.1.call-start = ((), (), s32[]{:S(2)}) async-start(), calls=%async_computation.6 | async-start | bytes 6389760 | tf_op jit(solution)/shard_map/all_gather | solution.py:150
  250.4 84.7 %copy-start.2 = (s32[1,512]{1,0:T(1,128)S(1)}, s32[1,512]{1,0:T(1,128)}, u32[]{:S(2)}) copy-start(s32[1,512]{1,0:T(1,128)} %param.21) | copy-start | bytes 6148
  250.5 91.6 %copy-start.3 = (s32[1,16]{1,0:T(1,128)S(1)}, s32[1,16]{1,0:T(1,128)}, u32[]{:S(2)}) copy-start(s32[1,16]{1,0:T(1,128)} %param.22) | copy-start | bytes 196
  335.2 33.5 %copy-start.1 = (s32[1,16]{1,0:T(1,128)S(1)}, s32[1,16]{1,0:T(1,128)}, u32[]{:S(2)}) copy-start(s32[1,16]{1,0:T(1,128)} %param.23) | copy-start | bytes 196
  336.2 23.5 %all-to-all-start.2 = ((f32[64,3,512]{2,1,0:T(4,128)}), f32[64,3,512]{2,1,0:T(4,128)}, u32[]{:S(2)}, u32[]{:S(2)}) async-start(f32[64,3,512]{2,1,0:T(4,128)} %broadcast_in_dim.84), calls=%async_computation.3 | async-start | bytes 1048576 | tf_op jit(solution)/shard_map/all_to_all | solution.py:11
Sparse Core Ops, SparseCore 0:
  40.2 58.6 all-gather.2
  126.5 100.7 reduce-scatter.1
  250.5 79.0 all-gather.4
where the time goes:
time: 377 us; the launch traced here: 376 us
  waiting for transfers between devices  256 us (68%)
  blocking collectives  40.6 us (11%)
  matrix products  37.3 us (10%)
  between operations  14 us (4%)
  local copies, waits for them, and re-layouts  13.1 us (3%)
  other arithmetic  9.63 us (3%)
  starting transfers between devices  5.98 us (2%)
    reduce_scatter x1, waiting for transfers between devices, on_device(): lax.psum_scatter(jnp.dot(hidden, down_rows, preferred_element_type=jnp.fl...  101 us
    all_gather x1, waiting for transfers between devices, on_device(): lax.all_gather(normed_out, ('expert', 'vocab'), axis=0, tiled=True)  79.1 us
    all_gather x1, waiting for transfers between devices, on_device(): lax.all_gather(arrived, ('vocab', 'batch'), axis=0, tiled=True)  58.8 us
    all_to_all x1, blocking collectives, on_device(): lax.all_to_all(buckets, 'expert', split_axis=0, concat_axis=0, tiled=True)  22.4 us
    dot_general x1, matrix products, on_device(): jnp.dot(hidden, down_rows, preferred_element_type=jnp.float32)  19.4 us
    all_to_all x1, blocking collectives, on_device(): lax.all_to_all(outgoing, 'expert', split_axis=0, concat_axis=0, tiled=True)  18.1 us
    all_to_all x1, waiting for transfers between devices, copy_for_each(): lax.all_to_all(jnp.broadcast_to(array[None], (peers, *array.shape)), axis...  16.9 us
    dot_general x1, matrix products, expand_rows(): jnp.dot(block_rows, gate_cols, preferred_element_type=jnp.float32)  8.09 us
  transfers between devices with their start and end apart: 4, of which 4 were waited for; matrix products, arithmetic and copies ran while one was open for 0% of the time, Pallas kernels for 0%

commit v1 on v0

--- a/solution.py
+++ b/solution.py
@@ -2,8 +2,13 @@
 import jax.numpy as jnp
 from jax import lax
 from jax.sharding import PartitionSpec as P
+from jax.lax import all_to_all, axis_size
 
 epsilon = 1e-05
+perform_shifts_all_on_mesh = lambda tile_in, array_dim: jnp.concatenate(
+    all_to_all(jnp.stack(axis_size(("vocab", "batch")) * [tile_in]), ("vocab", "batch"), 0, 0),
+    axis=array_dim,
+)
 
 
 def copy_for_each(array, axis):
@@ -127,9 +132,7 @@
     arrived = lax.all_to_all(buckets, "expert", split_axis=0, concat_axis=0, tiled=True).reshape(
         -1, model_width
     )
-    hidden = expand_rows(
-        lax.all_gather(arrived, ("vocab", "batch"), axis=0, tiled=True), gate_cols, up_cols
-    )
+    hidden = expand_rows(perform_shifts_all_on_mesh(arrived, 0), gate_cols, up_cols)
     expert_sum = lax.psum_scatter(
         jnp.dot(hidden, down_rows, preferred_element_type=jnp.float32).astype(jnp.bfloat16),
         ("vocab", "batch"),

time: 377 us -> 428 us (1.14)
  blocking collectives: 40.6 us -> 156 us
  waiting for transfers between devices: 256 us -> 191 us
  matrix products: 37.3 us -> 32.7 us
    all_to_all x0 -> x1, blocking collectives: none -> 115 us  [all_to_all(jnp.stack(axis_size(('vocab', 'batch')) * [tile_in]), ('vocab'...]
    all_gather x1 -> x0, waiting for transfers between devices: 58.8 us -> none  [on_device(): lax.all_gather(arrived, ('vocab', 'batch'), axis=0, tiled=True)]
    reduce_scatter x1, waiting for transfers between devices: 101 us -> 95.2 us  [on_device(): lax.psum_scatter(jnp.dot(hidden, down_rows, preferred_element_type=jnp.fl...]
    dot_general x1, matrix products: 8.09 us -> 3.55 us  [expand_rows(): jnp.dot(block_rows, gate_cols, preferred_element_type=jnp.float32)]
  transfers between devices with their start and end apart: 4 -> 3, of which waited for: 4 -> 3; matrix products, arithmetic and copies ran while one was open for 0% -> 0% of each run, Pallas kernels for 0% -> 0%
where the time goes in v1:
time: 428 us; the launch traced here: 427 us
  waiting for transfers between devices  191 us (45%)
  blocking collectives  156 us (36%)
  matrix products  32.7 us (8%)
  local copies, waits for them, and re-layouts  17.2 us (4%)
  between operations  14.3 us (3%)
  other arithmetic  9.63 us (2%)
  starting transfers between devices  5.92 us (1%)
    all_to_all x1, blocking collectives, all_to_all(jnp.stack(axis_size(('vocab', 'batch')) * [tile_in]), ('vocab'...  115 us
    reduce_scatter x1, waiting for transfers between devices, on_device(): lax.psum_scatter(jnp.dot(hidden, down_rows, preferred_element_type=jnp.fl...  95.2 us
    all_gather x1, waiting for transfers between devices, on_device(): lax.all_gather(normed_out, ('expert', 'vocab'), axis=0, tiled=True)  79.2 us
    all_to_all x1, blocking collectives, on_device(): lax.all_to_all(buckets, 'expert', split_axis=0, concat_axis=0, tiled=True)  22.4 us
    dot_general x1, matrix products, on_device(): jnp.dot(hidden, down_rows, preferred_element_type=jnp.float32)  19.4 us
    all_to_all x1, blocking collectives, on_device(): lax.all_to_all(outgoing, 'expert', split_axis=0, concat_axis=0, tiled=True)  18.1 us
    all_to_all x1, waiting for transfers between devices, copy_for_each(): lax.all_to_all(jnp.broadcast_to(array[None], (peers, *array.shape)), axis...  16.9 us
  transfers between devices with their start and end apart: 3, of which 3 were waited for; matrix products, arithmetic and copies ran while one was open for 0% of the time, Pallas kernels for 0%

profile of v1, /device:TPU:1, one launch (start us, length us, event | category | flops | bytes accessed | tf_op | source)
XLA Modules:
  0.0 427.0 jit_solution(11019909115493849214)
XLA Ops:
  7.2 0.9 copy.31
  8.1 0.1 eq.72
  8.2 0.1 fusion.28
  8.3 0.2 select_reduce_fusion.4
  8.5 0.1 reduce_sum.106
  8.6 0.1 copy.32
  8.7 0.7 multiply_add_fusion.5
  9.4 1.1 fusion.19
  10.4 1.2 fusion.24
  11.6 0.8 select_reduce_fusion.3
  12.5 0.1 convert_reduce_fusion
  12.6 1.9 convolution_convert_fusion.1
  14.5 1.1 reshape.130
  15.6 22.4 %all_to_all.20 = bf16[8,3,6144]{2,1,0:T(4,128)(2,1)} all-to-all(bf16[8,3,6144]{2,1,0:T(4,128)(2,1)S(1)} %reshape.130), channel_id=1, replica_groups=mesh['expert'=8,'vocab'=8,'batch'=4] {'expert'}, dimensions={0} | all-to-all | bytes 589824 | tf_op jit(solution)/shard_map/all_to_all | solution.py:132
  38.0 1.2 stack_reshape.2
  39.3 1.2 stack.3
  40.5 115.4 %all_to_all.21 = bf16[32,24,6144]{2,1,0:T(8,128)(2,1)S(1)} all-to-all(bf16[32,24,6144]{2,1,0:T(8,128)(2,1)S(1)} %stack.3), channel_id=1, replica_groups=mesh['expert'=8,'vocab'=8,'batch'=4] {'vocab','batch'}, dimensions={0} | all-to-all | bytes 18874368 | tf_op jit(solution)/shard_map/all_to_all | solution.py:9
  155.9 3.7 copy-done.1
  159.5 3.5 fusion.3
  163.1 19.4 %convolution_convert_fusion = bf16[768,6144]{1,0:T(8,128)(2,1)} fusion(bf16[1,256,6144]{2,1,0:T(8,128)(2,1)S(1)} %copy-done, bf16[768,6144]{1,0:T(8,128)(2,1)} %bitcast.65, bf16[1,6144,256]{2,1,0:T(8,128)(2,1)} %param.17, f32[768,256]{1,0:T(8,128)} %fusion.3), kind=kOutput, calls=%fused_computation | convolution fusion | flops 4837736448 | bytes 25952256 | tf_op jit(solution)/shard_map/dot_general | solution.py:137
  182.5 95.2 %reduce-scatter.2.cloned.1.call-done = bf16[24,6144]{1,0:T(8,128)(2,1)} async-done(((bf16[768,6144]{1,0:T(8,128)(2,1)}), bf16[24,6144]{1,0:T(8,128)(2,1)}) %reduce-scatter.2.cloned.1.call-update) | async-done | bytes 294928 | tf_op jit(solution)/shard_map/reduce_scatter | solution.py:136
  277.8 1.1 reshape.132
  278.9 18.1 %all_to_all.22 = bf16[8,3,6144]{2,1,0:T(4,128)(2,1)} all-to-all(bf16[8,3,6144]{2,1,0:T(4,128)(2,1)S(1)} %reshape.132), channel_id=1, replica_groups=mesh['expert'=8,'vocab'=8,'batch'=4] {'expert'}, dimensions={0} | all-to-all | bytes 589824 | tf_op jit(solution)/shard_map/all_to_all | solution.py:143
  297.0 1.2 reshape.133
  298.2 1.2 multiply_reduce_fusion
  299.4 1.5 multiply_convert_fusion
  301.0 79.2 %all-gather.2.cloned.1.call-done = bf16[512,6144]{1,0:T(8,128)(2,1)} async-done(((bf16[8,6144]{1,0:T(8,128)(2,1)}), bf16[512,6144]{1,0:T(8,128)(2,1)}) %all-gather.2.cloned.1.call-update) | async-done | bytes 6291472 | tf_op jit(solution)/shard_map/all_gather | solution.py:153
  380.2 5.5 %fusion.37 = (f32[512]{0:T(512)S(1)}, f32[512,256]{0,1:T(8,128)S(1)}) fusion(bf16[512,6144]{1,0:T(8,128)(2,1)} %all-gather.2.cloned.1.call-done, bf16[256,6144]{1,0:T(8,128)(2,1)} %param.19), kind=kOutput, calls=%fused_computation.74 | convolution fusion | flops 1610743296 | bytes 9963520 | tf_op jit(solution)/shard_map/dot_general | solution.py:152
  385.8 0.1 exponential_reduce_fusion
  385.9 0.9 broadcast_in_dim.84
  386.8 5.8 %all-to-all-start.3 = ((f32[64,3,512]{2,1,0:T(4,128)}), f32[64,3,512]{2,1,0:T(4,128)}, u32[]{:S(2)}, u32[]{:S(2)}) async-start(f32[64,3,512]{2,1,0:T(4,128)} %broadcast_in_dim.84), calls=%async_computation.4 | async-start | bytes 1048576 | tf_op jit(solution)/shard_map/all_to_all | solution.py:16
  392.7 0.1 copy.35
  392.8 0.1 reduce
  392.9 0.5 bitcast_subtract_fusion.1
  393.4 16.9 %all-to-all-done.3 = f32[64,3,512]{2,1,0:T(4,128)} async-done(((f32[64,3,512]{2,1,0:T(4,128)}), f32[64,3,512]{2,1,0:T(4,128)}, u32[]{:S(2)}, u32[]{:S(2)}) %all-to-all-start.3) | async-done | bytes 393248 | tf_op jit(solution)/shard_map/all_to_all | solution.py:16
  410.3 1.8 fusion.36
  412.1 0.6 slice.124
  412.7 0.6 slice.125
  413.4 0.9 add.97
  414.6 0.6 slice.138
  415.2 0.6 slice.137
  415.8 0.9 multiply_add_fusion
  417.2 0.6 constant_dynamic-slice_fusion
  417.8 0.8 select_reduce_fusion.1
  418.6 0.7 bitcast_divide_fusion.1
  419.3 0.2 fusion.26
  419.5 0.2 fusion.27
  419.7 0.5 bitcast_divide_fusion
  (61 shorter events, 1.0 us)
Async XLA Ops:
  7.2 155.9 %copy-start = (bf16[1,256,6144]{2,1,0:T(8,128)(2,1)S(1)}, bf16[1,256,6144]{2,1,0:T(8,128)(2,1)}, u32[]{:S(2)}) copy-start(bf16[1,256,6144]{2,1,0:T(8,128)(2,1)} %param.18) | copy-start | bytes 9437188
  7.2 270.6 %reduce-scatter.2.cloned.1.call-start = ((), (), s32[]{:S(2)}) async-start(), calls=%async_computation.5 | async-start | bytes 9732096 | tf_op jit(solution)/shard_map/reduce_scatter | solution.py:136
  40.5 119.1 %copy-start.5 = (bf16[1,6144,256]{2,1,0:T(8,128)(2,1)S(1)}, bf16[1,6144,256]{2,1,0:T(8,128)(2,1)}, u32[]{:S(2)}) copy-start(bf16[1,6144,256]{2,1,0:T(8,128)(2,1)} %param.16) | copy-start | bytes 9437188
  155.9 3.7 copy-start.1
  182.5 197.7 %all-gather.2.cloned.1.call-start = ((), (), s32[]{:S(2)}) async-start(), calls=%async_computation.6 | async-start | bytes 6389760 | tf_op jit(solution)/shard_map/all_gather | solution.py:153
  300.9 84.8 %copy-start.3 = (s32[1,512]{1,0:T(1,128)S(1)}, s32[1,512]{1,0:T(1,128)}, u32[]{:S(2)}) copy-start(s32[1,512]{1,0:T(1,128)} %param.21) | copy-start | bytes 6148
  300.9 91.7 %copy-start.4 = (s32[1,16]{1,0:T(1,128)S(1)}, s32[1,16]{1,0:T(1,128)}, u32[]{:S(2)}) copy-start(s32[1,16]{1,0:T(1,128)} %param.22) | copy-start | bytes 196
  385.8 33.5 %copy-start.2 = (s32[1,16]{1,0:T(1,128)S(1)}, s32[1,16]{1,0:T(1,128)}, u32[]{:S(2)}) copy-start(s32[1,16]{1,0:T(1,128)} %param.23) | copy-start | bytes 196
  386.8 23.5 %all-to-all-start.3 = ((f32[64,3,512]{2,1,0:T(4,128)}), f32[64,3,512]{2,1,0:T(4,128)}, u32[]{:S(2)}, u32[]{:S(2)}) async-start(f32[64,3,512]{2,1,0:T(4,128)} %broadcast_in_dim.84), calls=%async_computation.4 | async-start | bytes 1048576 | tf_op jit(solution)/shard_map/all_to_all | solution.py:16
Sparse Core Ops, SparseCore 0:
  182.6 95.1 reduce-scatter.1
  301.0 79.1 all-gather.1
